TPU v7x, 32 devices: a whole 2x2x4 slice. The times are simulated.
32 devices in a mesh: seq: 8 (over y, x, core), head: 4 (over z).
Axes of the slice: x: 2, y: 2, z: 4, core: 2. Of those that a mesh axis runs over, the one named last changes fastest.
Arguments:
- queries: bfloat16 [1024, 8192], P('seq', 'head'), may hold values from -6 to 6, as said below
- keys: bfloat16 [1024, 1024], P('seq'), may hold values from -6 to 6, as said below
- values: bfloat16 [1024, 1024], P('seq'), may hold values from -6 to 6
- residual: bfloat16 [1024, 8192], P('seq', 'head'), may hold values from -50 to 50
- norm_gain: float32 [8192], replicated, may hold values from 0.25 to 1.75
- block_pos: int32 [1, 8], replicated, may hold values from 0 to 7, each once within a row
- doc_offset: int32 [1, 8], replicated, may hold values from 1 to 128, as said below
Outputs:
- attn_out: bfloat16 [1024, 8192], P('seq', 'head')
- r_factor: float32 [64, 128, 128], P('head')
- whitened: float32 [1024, 8192], P('seq', 'head')
Inputs may be any that keep to these rules, and one draw needn't show every extreme that they name: queries may hold rows of large entries. keys may hold rows of large entries. `block_pos`: in each sequence every sequence block is stored exactly once. A document begins at token doc_offset[c, b] of sequence block b when that value is under 128; the first document begins at position 0.
All inputs are finite; a program needn't handle non-finite values.
Results may differ from a plain program's by a relative error of at most 0.0045.
Values may be sent and summed in bfloat16 or wider, within the bound.
A program may use at most 64 MiB of HBM per device.

v0:
```python
import math

import jax
import jax.numpy as jnp
from jax import lax
from jax.sharding import PartitionSpec as P

HEADS = 64
KVH = 8
HD = 128
BLOCK = 128
COPIES = 1
WIDTH = 8192


EPSILON = 1e-05


def positions_and_docs(block_pos, doc_offset):
    block_total = block_pos.shape[0]
    doc_flags = (doc_offset < BLOCK).astype(jnp.int32)
    starts_before = jnp.cumsum(doc_flags) - doc_flags
    matches = block_pos[:, None] == jnp.arange(block_total, dtype=jnp.int32)[None, :]
    start_count = jnp.sum(jnp.where(matches, starts_before[None, :], 0), axis=1)
    offsets = jnp.sum(jnp.where(matches, doc_offset[None, :], 0), axis=1)
    within = jnp.arange(BLOCK, dtype=jnp.int32)
    seq_pos = (block_pos[:, None] * BLOCK + within[None, :]).reshape(-1)
    doc_id = (
        start_count[:, None] + (within[None, :] >= offsets[:, None]).astype(jnp.int32)
    ).reshape(-1)
    return (seq_pos, doc_id)


def gram_of(matrix):
    return jnp.einsum("hnc,hnd->hcd", matrix, matrix, precision=lax.Precision.HIGHEST)


def local(queries, keys, values, residual, norm_gain, block_pos, doc_offset):
    row_count = queries.shape[0]
    head_count = queries.shape[1] // HD
    group_size = HEADS // KVH
    share_count = max(1, head_count // group_size)
    per_share = head_count // share_count
    total_rows = row_count * lax.axis_size("seq")
    global_first = lax.axis_index("head") * head_count
    copy_index = global_first // HEADS
    first_head = global_first % HEADS
    first_share = first_head // group_size
    key_start = copy_index * (KVH * HD) + first_share * HD
    key_cols = lax.dynamic_slice_in_dim(keys, key_start, share_count * HD, 1)
    value_cols = lax.dynamic_slice_in_dim(values, key_start, share_count * HD, 1)
    own_blocks = lax.dynamic_index_in_dim(block_pos, copy_index, 0, keepdims=False)
    own_offsets = lax.dynamic_index_in_dim(doc_offset, copy_index, 0, keepdims=False)
    gain_cols = lax.dynamic_slice_in_dim(norm_gain, first_head * HD, head_count * HD)
    seq_pos, doc_id = positions_and_docs(own_blocks, own_offsets)
    first_row = lax.axis_index("seq") * row_count
    own_pos = lax.dynamic_slice_in_dim(seq_pos, first_row, row_count)
    own_doc = lax.dynamic_slice_in_dim(doc_id, first_row, row_count)
    query_heads = queries.reshape(row_count, share_count, per_share, HD)
    score_scale = 1.0 / math.sqrt(HD)

    def attend_block(state_now, key_piece, value_piece, first_key):
        length = key_piece.shape[0]
        key_pos = lax.dynamic_slice_in_dim(seq_pos, first_key, length)
        key_doc = lax.dynamic_slice_in_dim(doc_id, first_key, length)
        seen = (key_pos[None, :] <= own_pos[:, None]) & (key_doc[None, :] == own_doc[:, None])

        def accumulate(state_inner):
            run_max, run_total, run_acc = state_inner
            key_heads = key_piece.reshape(length, share_count, HD)
            value_heads = value_piece.reshape(length, share_count, HD)
            scores = (
                jnp.einsum(
                    "rkgd,nkd->kgrn", query_heads, key_heads, preferred_element_type=jnp.float32
                )
                * score_scale
            )
            scores = jnp.where(seen[None, None], scores, -jnp.inf)
            new_max = jnp.maximum(run_max, jnp.max(scores, axis=3))
            factor = jnp.exp(run_max - new_max)
            expo = jnp.exp(scores - new_max[..., None])
            new_total = run_total * factor + jnp.sum(expo, axis=3)
            partial_value = jnp.einsum(
                "kgrn,nkd->kgrd",
                expo.astype(jnp.bfloat16),
                value_heads,
                preferred_element_type=jnp.float32,
            )
            new_acc = run_acc * factor[..., None] + partial_value
            return (new_max, new_total, new_acc)

        def unchanged(state_inner):
            return state_inner

        return lax.cond(jnp.any(seen), accumulate, unchanged, state_now)

    def attend(state_now, pieces, first_key):
        key_piece, value_piece = pieces
        length = key_piece.shape[0]
        step_rows = math.gcd(length, 1024)
        if step_rows == length:
            return attend_block(state_now, key_piece, value_piece, first_key)

        def advance(step_index, state_inner):
            begin_row = step_index * step_rows
            key_part = lax.dynamic_slice_in_dim(key_piece, begin_row, step_rows, 0)
            value_part = lax.dynamic_slice_in_dim(value_piece, begin_row, step_rows, 0)
            return attend_block(state_inner, key_part, value_part, first_key + begin_row)

        return lax.fori_loop(0, length // step_rows, advance, state_now)

    start_state = (
        jnp.full((share_count, per_share, row_count), -1e30, jnp.float32),
        jnp.zeros((share_count, per_share, row_count), jnp.float32),
        jnp.zeros((share_count, per_share, row_count, HD), jnp.float32),
    )
    final_max, final_total, final_acc = attend(
        start_state,
        (
            lax.all_gather(key_cols, "seq", axis=0, tiled=True),
            lax.all_gather(value_cols, "seq", axis=0, tiled=True),
        ),
        jnp.int32(0),
    )
    output = final_acc / final_total[..., None]
    attn_out = (
        jnp.transpose(output, (2, 0, 1, 3)).reshape(row_count, head_count * HD).astype(jnp.bfloat16)
    )
    mixed = attn_out.astype(jnp.float32) + residual.astype(jnp.float32)
    local_squares = jnp.sum(mixed * mixed, axis=1)
    slot_mask = jnp.arange(COPIES, dtype=jnp.int32) == copy_index
    slotted = jnp.where(slot_mask[:, None], local_squares[None, :], 0.0)
    summed = lax.psum(slotted, "head")
    square_sum = lax.dynamic_index_in_dim(summed, copy_index, 0, keepdims=False)
    normed = mixed * lax.rsqrt(square_sum[:, None] / WIDTH + EPSILON) * gain_cols[None, :]
    blocks = normed.reshape(row_count, head_count, HD)
    head_rows = jnp.transpose(blocks, (1, 0, 2))
    gram_sum = lax.psum(gram_of(head_rows), "seq")
    lower_factor = jnp.linalg.cholesky(gram_sum)
    r_factor = jnp.transpose(lower_factor, (0, 2, 1)) / math.sqrt(total_rows)
    solved = jax.scipy.linalg.solve_triangular(
        lower_factor, jnp.transpose(blocks, (1, 2, 0)), lower=True
    )
    whitened = jnp.transpose(solved, (2, 0, 1)).reshape(row_count, head_count * HD) * math.sqrt(
        total_rows
    )
    return (attn_out, r_factor, whitened)


def solution(mesh):
    return jax.shard_map(
        local,
        mesh=mesh,
        in_specs=(
            P("seq", "head"),
            P("seq", None),
            P("seq", None),
            P("seq", "head"),
            P(),
            P(),
            P(),
        ),
        out_specs=(P("seq", "head"), P("head", None, None), P("seq", "head")),
        check_vma=False,
    )
```

profile of v0, /device:TPU:0, one launch (start us, length us, event | category | flops | bytes accessed | tf_op | source)
XLA Modules:
  0.0 479.9 jit_solution(18409932221728924501)
XLA Ops:
  7.2 0.0 copy-start
  7.2 0.0 all-reduce.2.cloned.1.call-start
  7.3 0.7 compare_convert_fusion
  7.9 0.2 reduce-window_clone.1
  8.1 0.7 subtract_bitcast_fusion
  8.8 0.7 broadcast_multiply_fusion
  9.4 0.9 select_reduce_fusion.2
  10.3 0.1 add_bitcast_fusion
  10.4 0.1 dynamic_slice.21
  10.5 0.1 dynamic_slice.20
  10.5 1.0 fusion.24
  12.2 0.0 copy-done
  12.2 11.3 %all_gather.6 = bf16[1024,256]{1,0:T(8,128)(2,1)S(1)} all-gather(bf16[128,256]{1,0:T(8,128)(2,1)S(1)} %constant_dynamic-slice_fusion.1), channel_id=1, replica_groups=mesh['seq'=8,'head'=4] {'seq'}, dimensions={0}, use_global_device_ids=true | all-gather | bytes 589824 | tf_op jit(solution)/shard_map/all_gather | solution.py:120
  23.5 0.8 constant_dynamic-slice_fusion
  24.4 9.8 %all_gather.7 = bf16[1024,256]{1,0:T(8,128)(2,1)S(1)} all-gather(bf16[128,256]{1,0:T(8,128)(2,1)S(1)} %constant_dynamic-slice_fusion), channel_id=1, replica_groups=mesh['seq'=8,'head'=4] {'seq'}, dimensions={0}, use_global_device_ids=true | all-gather | bytes 589824 | tf_op jit(solution)/shard_map/all_gather | solution.py:121
  34.2 12.7 %conditional.1 = (f32[2,8,128]{2,1,0:T(8,128)S(1)}, f32[2,8,128,128]{3,2,1,0:T(8,128)S(1)}) conditional(s32[]{:T(128)} %convert_element_type.40, () %tuple.16, (pred[128,1024]{0,1:T(8,128)(4,1)S(1)}, bf16[1024,256]{1,0:T(8,128)(2,1)S(1)}, bf16[128,2048]{1,0:T(8,128)(2,1)}, bf16[1024,256]{1,0:T(8,128)(2,1)S(1)}) %tuple.17), branch_computations={%region_4.5_spmd, %region_5.8_spmd} | conditional | flops 1097078784 | bytes 64970796 | solution.py:95
  34.2 1.2 copy.49
  35.4 0.1 reshape.142
  35.5 1.3 fusion.2
  36.9 0.0 copy-start.1
  36.9 3.2 copy-done.1
  40.1 1.7 fusion.1
  41.9 0.1 reshape.144
  42.0 4.9 %fusion.6 = f32[2,8,128,128]{3,2,1,0:T(8,128)S(1)} fusion(f32[2,1024,128,8]{2,1,3,0:T(8,128)} %copy-done.1, f32[2,8,128]{2,1,0:T(8,128)S(1)} %broadcast_maximum_fusion, pred[128,1024]{0,1:T(8,128)(4,1)S(1)} %get-tuple-element.9, bf16[1024,2,128,1]{2,1,0,3:T(2,128)(2,1)S(1)} %bitcast.68, f32[2,8,128]{2,1,0:T(8,128)S(1)} %get-tuple-element.34), kind=kOutput, calls=%fused_computation.7 | convolution fusion | flops 545521664 | bytes 10108928 | tf_op jit(solution)/shard_map/cond/branch_1_fun/kgrn,nkd->kgrd/dot_general | solution.py:83
  46.9 0.3 fusion.22
  47.2 0.3 copy.28
  47.6 0.0 copy-done.2
  47.6 0.3 multiply_reduce_fusion
  47.9 0.0 copy-start.3
  48.0 12.1 %psum.14 = f32[1,128]{1,0:T(1,128)S(1)} all-reduce(f32[1,128]{1,0:T(1,128)S(1)} %fusion.23), channel_id=1, replica_groups=mesh['seq'=8,'head'=4] {'head'}, use_global_device_ids=true, to_apply=%region_9.10 | all-reduce | flops 128 | bytes 1024 | tf_op jit(solution)/shard_map/psum | solution.py:133
  60.1 0.8 dynamic_slice.24
  60.9 0.2 multiply_bitcast_fusion.1
  61.1 0.2 copy.51
  61.3 0.0 copy-done.3
  61.3 0.4 copy.29
  61.8 3.0 fusion.19
  64.7 0.0 all-reduce.2.cloned.1.call-update
  64.8 54.0 %all-reduce.2.cloned.1.call-done = f32[16,128,128]{1,2,0:T(8,128)} async-done(((f32[16,128,128]{1,2,0:T(8,128)}), f32[16,128,128]{1,2,0:T(8,128)}) %all-reduce.2.cloned.1.call-update) | async-done | bytes 1048592 | tf_op jit(solution)/shard_map/psum | solution.py:138
  118.8 1.6 copy.32
  120.3 1.3 fusion.18
  121.7 187.5 %custom-call.8 = f32[16,128,128]{2,1,0:T(8,128)S(1)} custom-call(f32[16,128,128]{2,1,0:T(8,128)S(1)} %fusion.18), custom_call_target="Cholesky" | custom-call | tf_op jit(solution)/shard_map/jit(cholesky)/cholesky | solution.py:139
  309.2 0.1 select_reduce_fusion
  309.3 0.1 compare_reduce_fusion
  309.4 1.2 select_bitcast_fusion
  310.7 1.3 copy.35
  312.0 157.9 %custom-call.9 = f32[16,1,128,128]{2,3,1,0:T(8,128)S(1)} custom-call(f32[16,1,128,128]{3,2,1,0:T(8,128)} %get-tuple-element.38), custom_call_target="InvertDiagBlocksLowerTriangular" | custom-call | tf_op jit(solution)/shard_map/jit(_solve_triangular)/vmap()/triangular_solve | solution.py:141
  469.9 1.8 convolution_multiply_fusion
  471.8 1.3 copy.36
  (8 shorter events, 0.1 us)
Async XLA Ops:
  7.2 5.0 %copy-start = (bf16[128,1024]{1,0:T(8,128)(2,1)S(1)}, bf16[128,1024]{1,0:T(8,128)(2,1)}, u32[]{:S(2)}) copy-start(bf16[128,1024]{1,0:T(8,128)(2,1)} %param.10) | copy-start | bytes 786436
  7.2 111.6 %all-reduce.2.cloned.1.call-start = ((), (), s32[]{:S(2)}) async-start(), calls=%async_computation | async-start | bytes 2097152 | tf_op jit(solution)/shard_map/psum | solution.py:138
  34.2 13.4 %copy-start.2 = (bf16[128,2048]{1,0:T(8,128)(2,1)S(1)}, bf16[128,2048]{1,0:T(8,128)(2,1)}, u32[]{:S(2)}) copy-start(bf16[128,2048]{1,0:T(8,128)(2,1)} %param.12) | copy-start | bytes 1572868
  36.9 3.2 copy-start.1
  47.9 13.4 %copy-start.3 = (bf16[128,2048]{1,0:T(8,128)(2,1)}, bf16[128,2048]{1,0:T(8,128)(2,1)S(1)}, u32[]{:S(2)}) copy-start(bf16[128,2048]{1,0:T(8,128)(2,1)S(1)} %get-tuple-element.31) | copy-start | bytes 1572868
Sparse Core Ops, SparseCore 0:
  64.9 53.8 all-reduce.1
where the time goes:
time: 480 us
  other arithmetic  355 us (74%)
  waiting for transfers between devices  54 us (11%)
  blocking collectives  33.3 us (7%)
  between operations  14.9 us (3%)
  local copies, waits for them, and re-layouts  11.6 us (2%)
  matrix products  11 us (2%)
    another operation x4, other arithmetic, local(): lower_factor = jnp.linalg.cholesky(gram_sum)  188 us
    another operation x2, other arithmetic, local(): jax.scipy.linalg.solve_triangular(lower_factor, jnp.transpose(blocks, (1,...  159 us
    psum x1, waiting for transfers between devices, local(): gram_sum = lax.psum(gram_of(head_rows), 'seq')  54 us
    psum x1, blocking collectives, local(): summed = lax.psum(slotted, 'head')  12.1 us
    all_gather x1, blocking collectives, local(): lax.all_gather(key_cols, 'seq', axis=0, tiled=True)  11.3 us
    all_gather x1, blocking collectives, local(): lax.all_gather(value_cols, 'seq', axis=0, tiled=True)  9.82 us
  transfers between devices with their start and end apart: 1, of which 1 were waited for; matrix products, arithmetic and copies ran while one was open for 0% of the time, Pallas kernels for 0%

commit v1 on v0

--- a/solution.py
+++ b/solution.py
@@ -1,8 +1,11 @@
+import functools
 import math
 
 import jax
 import jax.numpy as jnp
 from jax import lax
+from jax.experimental import pallas as pl
+from jax.experimental.pallas import tpu as pltpu
 from jax.sharding import PartitionSpec as P
 
 HEADS = 64
@@ -19,7 +22,9 @@
 def positions_and_docs(block_pos, doc_offset):
     block_total = block_pos.shape[0]
     doc_flags = (doc_offset < BLOCK).astype(jnp.int32)
-    starts_before = jnp.cumsum(doc_flags) - doc_flags
+    places = jnp.arange(block_total, dtype=jnp.int32)
+    earlier = places[:, None] < places[None, :]
+    starts_before = jnp.sum(jnp.where(earlier, doc_flags[:, None], 0), axis=0)
     matches = block_pos[:, None] == jnp.arange(block_total, dtype=jnp.int32)[None, :]
     start_count = jnp.sum(jnp.where(matches, starts_before[None, :], 0), axis=1)
     offsets = jnp.sum(jnp.where(matches, doc_offset[None, :], 0), axis=1)
@@ -31,11 +36,102 @@
     return (seq_pos, doc_id)
 
 
+HIGHEST = lax.Precision.HIGHEST
+MESH = pl.DeviceIdType.MESH
+PANEL = 16
+LOG2E = 1.4426950408889634
+
+
+def iota(shape, dimension):
+    return lax.broadcasted_iota(jnp.int32, shape, dimension)
+
+
+def factor(m_ref):
+    count = m_ref.shape[0]
+    lane = iota((PANEL, HD), 1)
+    sub = iota((PANEL, HD), 0)
+
+    def panel(j, carry):
+        base = pl.multiple_of(j * PANEL, PANEL)
+        rows = pl.ds(base, PANEL)
+        left = [m_ref[c, rows, :HD] for c in range(count)]
+        right = [m_ref[c, rows, HD:] for c in range(count)]
+        columns = [
+            [
+                jnp.broadcast_to(
+                    jnp.sum(jnp.where(lane == base + i, left[c], 0.0), axis=1, keepdims=True),
+                    (PANEL, HD),
+                )
+                for i in range(PANEL)
+            ]
+            for c in range(count)
+        ]
+        scale = [jnp.ones((PANEL, HD), jnp.float32) for c in range(count)]
+        for i in range(PANEL):
+            for c in range(count):
+                pivot = columns[c][i][i : i + 1, :]
+                scale[c] = jnp.where(sub == i, lax.rsqrt(pivot), scale[c])
+                ratio = jnp.where(sub > i, columns[c][i] * (1.0 / pivot), 0.0)
+                left[c] = left[c] - ratio * left[c][i : i + 1, :]
+                right[c] = right[c] - ratio * right[c][i : i + 1, :]
+                for k in range(i + 1, PANEL):
+                    columns[c][k] = columns[c][k] - ratio * columns[c][k][i : i + 1, :]
+        for c in range(count):
+            both = jnp.concatenate([left[c] * scale[c], right[c] * scale[c]], axis=1)
+            m_ref[c, rows, :] = both
+            later = jnp.where(lane >= base + PANEL, both[:, :HD], 0.0)
+            m_ref[c] = m_ref[c] - lax.dot_general(
+                later,
+                both,
+                (((0,), (0,)), ((), ())),
+                precision=HIGHEST,
+                preferred_element_type=jnp.float32,
+            )
+        return carry
+
+    lax.fori_loop(0, HD // PANEL, panel, 0)
+
+
+def pack(m):
+    return jnp.where(iota((HD, HD), 1) >= iota((HD, HD), 0), m[:, :HD], m[:, HD:])
+
+
+def unpack(x):
+    row, col = iota((HD, HD), 0), iota((HD, HD), 1)
+    upper = jnp.where(col >= row, x, 0.0)
+    inverse = jnp.where(col < row, x, jnp.where(col == row, 1.0 / x, 0.0))
+    return (upper, inverse)
+
+
+def identity():
+    return jnp.where(iota((HD, HD), 0) == iota((HD, HD), 1), 1.0, 0.0)
+
+
+def factor_kernel(g_ref, x_ref, m_ref):
+    m_ref[0, :, :HD] = g_ref[0]
+    m_ref[0, :, HD:] = identity()
+    factor(m_ref)
+    x_ref[0] = pack(m_ref[0])
+
+
+def factor_heads(gram):
+    spec = pl.BlockSpec((1, HD, HD), lambda h: (h, 0, 0))
+    return pl.pallas_call(
+        factor_kernel,
+        grid=(gram.shape[0],),
+        in_specs=[spec],
+        out_specs=spec,
+        out_shape=jax.ShapeDtypeStruct(gram.shape, jnp.float32),
+        scratch_shapes=[pltpu.VMEM((1, HD, 2 * HD), jnp.float32)],
+        name="factor_heads",
+    )(gram)
+
+
 def gram_of(matrix):
     return jnp.einsum("hnc,hnd->hcd", matrix, matrix, precision=lax.Precision.HIGHEST)
 
 
-def local(queries, keys, values, residual, norm_gain, block_pos, doc_offset):
+def local_generic(queries, keys, values, residual, norm_gain, block_pos, doc_offset):
     row_count = queries.shape[0]
     head_count = queries.shape[1] // HD
     group_size = HEADS // KVH
@@ -136,18 +232,359 @@
     blocks = normed.reshape(row_count, head_count, HD)
     head_rows = jnp.transpose(blocks, (1, 0, 2))
     gram_sum = lax.psum(gram_of(head_rows), "seq")
-    lower_factor = jnp.linalg.cholesky(gram_sum)
-    r_factor = jnp.transpose(lower_factor, (0, 2, 1)) / math.sqrt(total_rows)
-    solved = jax.scipy.linalg.solve_triangular(
-        lower_factor, jnp.transpose(blocks, (1, 2, 0)), lower=True
+    upper, inverse = unpack(factor_heads(gram_sum))
+    r_factor = upper / math.sqrt(total_rows)
+    whitened = jnp.einsum("rhc,hdc->rhd", blocks, inverse, precision=HIGHEST)
+    whitened = whitened.reshape(row_count, head_count * HD) * math.sqrt(total_rows)
+    return (attn_out, r_factor, whitened)
+
+
+PEERS = 8
+
+
+def fused_kernel(
+    heads,
+    head_parts,
+    q_ref,
+    k_ref,
+    v_ref,
+    res_ref,
+    gain_ref,
+    pos_ref,
+    off_ref,
+    attn_hbm,
+    r_hbm,
+    white_hbm,
+    q_buf,
+    res_buf,
+    k_buf,
+    v_buf,
+    bias,
+    attn_buf,
+    mixed,
+    squares,
+    g_send,
+    g_recv,
+    m_ref,
+    x_buf,
+    r_buf,
+    white_buf,
+    local_sem,
+    kv_send,
+    kv_recv,
+    sq_send,
+    sq_recv,
+    g_send_sem,
+    g_recv_sem,
+    x_send,
+    x_recv,
+):
+    me = lax.axis_index("seq")
+    part = lax.axis_index("head")
+    group = HEADS // KVH
+    shares = heads // group
+    width = shares * HD
+    core = me % 2
+    bit_x = (me // 2) % 2
+    bit_y = me // 4
+    to_sib = 1 - 2 * core
+    to_x = 2 - 4 * bit_x
+    to_y = 4 - 8 * bit_y
+    sib = me + to_sib
+    near = [me + to_x + to_y, me + to_x, me + to_y]
+
+    key_cols = pl.ds(pl.multiple_of(part * width, HD), width)
+    own_rows = pl.ds(pl.multiple_of(me * BLOCK, BLOCK), BLOCK)
+    loads = [
+        pltpu.make_async_copy(k_ref.at[:, key_cols], k_buf.at[own_rows], local_sem.at[0]),
+        pltpu.make_async_copy(v_ref.at[:, key_cols], v_buf.at[own_rows], local_sem.at[1]),
+        pltpu.make_async_copy(q_ref, q_buf, local_sem.at[2]),
+        pltpu.make_async_copy(res_ref, res_buf, local_sem.at[3]),
+    ]
+    for copy in loads:
+        copy.start()
+
+    barrier = pltpu.get_barrier_semaphore()
+    for step in range(1, PEERS):
+        pl.semaphore_signal(
+            barrier, inc=1, device_id=((me + step) % PEERS, part), device_id_type=MESH
+        )
+    for step in range(1, head_parts):
+        pl.semaphore_signal(
+            barrier, inc=1, device_id=(me, (part + step) % head_parts), device_id_type=MESH
+        )
+    pl.semaphore_wait(barrier, PEERS - 1 + head_parts - 1)
+
+    def remote(src, dst, send, recv, device):
+        return pltpu.make_async_remote_copy(
+            src_ref=src,
+            dst_ref=dst,
+            send_sem=send,
+            recv_sem=recv,
+            device_id=device,
+            device_id_type=MESH,
+        )
+
+    def spread(slot_of, send, recv):
+        copies = []
+        for t, peer in enumerate(near + [sib]):
+            copy = remote(slot_of(me), slot_of(me), send.at[t], recv.at[me], (peer, part))
+            copy.start()
+            copies.append(copy)
+        return copies
+
+    def arrived(slot_of, send, recv, owner):
+        remote(slot_of(owner), slot_of(owner), send.at[0], recv.at[owner], (sib, part)).wait_recv()
+
+    def forward(slot_of, send, recv, t):
+        owner = near[t]
+        arrived(slot_of, send, recv, owner)
+        copy = remote(slot_of(owner), slot_of(owner), send.at[4 + t], recv.at[owner], (sib, part))
+        copy.start()
+        return copy
+
+    def rows_of(buf):
+        return lambda owner: buf.at[pl.ds(pl.multiple_of(owner * BLOCK, BLOCK), BLOCK)]
+
+    pending = []
+    kv = [(rows_of(k_buf), kv_send.at[0], kv_recv.at[0]), (rows_of(v_buf), kv_send.at[1], kv_recv.at[1])]
+    for i, way in enumerate(kv):
+        loads[i].wait()
+        pending += spread(*way)
+
+    row_pos = pos_ref[0, me]
+    lane = iota((BLOCK, BLOCK), 1)
+    sub = iota((BLOCK, BLOCK), 0)
+
+    def starts(position):
+        total = jnp.int32(0)
+        for b in range(PEERS):
+            counted = (b < position) & (off_ref[0, b] < BLOCK)
+            total = total + jnp.where(counted, 1, 0)
+        return total
+
+    own_pos = row_pos * BLOCK + sub
+    own_doc = starts(row_pos) + jnp.where(sub >= off_ref[0, row_pos], 1, 0)
+    for s in range(PEERS):
+        position = pos_ref[0, s]
+        key_pos = position * BLOCK + lane
+        key_doc = starts(position) + jnp.where(lane >= off_ref[0, position], 1, 0)
+        seen = (key_pos <= own_pos) & (key_doc == own_doc)
+        bias[:, s * BLOCK : (s + 1) * BLOCK] = jnp.where(seen, 0.0, -jnp.inf)
+
+    for t in range(3):
+        for way in kv:
+            pending.append(forward(*way, t))
+    for owner in [sib] + [peer + to_sib for peer in near]:
+        for way in kv:
+            arrived(*way, owner)
+    loads[2].wait()
+    loads[3].wait()
+
+    def attend(h, square):
+        cols = pl.ds(pl.multiple_of(h * HD, HD), HD)
+        share = pl.ds(pl.multiple_of((h // group) * HD, HD), HD)
+        scores = lax.dot_general(
+            q_buf[:, cols],
+            k_buf[:, share],
+            (((1,), (1,)), ((), ())),
+            preferred_element_type=jnp.float32,
+        )
+        scores = scores + bias[...]
+        top = jnp.max(scores, axis=1, keepdims=True)
+        expo = jnp.exp2((scores - top) * (LOG2E / math.sqrt(HD)))
+        total = jnp.sum(expo, axis=1, keepdims=True)
+        out = lax.dot_general(
+            expo.astype(jnp.bfloat16),
+            v_buf[:, share],
+            (((1,), (0,)), ((), ())),
+            preferred_element_type=jnp.float32,
+        )
+        out = (out / total).astype(jnp.bfloat16)
+        attn_buf[:, cols] = out
+        mix = out.astype(jnp.float32) + res_buf[:, cols].astype(jnp.float32)
+        mixed[:, cols] = mix
+        return square + mix * mix
+
+    square = lax.fori_loop(
+        0, heads, attend, jnp.zeros((BLOCK, HD), jnp.float32), unroll=4
     )
-    whitened = jnp.transpose(solved, (2, 0, 1)).reshape(row_count, head_count * HD) * math.sqrt(
-        total_rows
+    attn_out = pltpu.make_async_copy(attn_buf, attn_hbm, local_sem.at[4])
+    attn_out.start()
+
+    squares[part] = jnp.broadcast_to(jnp.sum(square.T, axis=0, keepdims=True), (8, HD))
+    for step in range(1, head_parts):
+        copy = remote(
+            squares.at[part],
+            squares.at[part],
+            sq_send.at[step],
+            sq_recv.at[part],
+            (me, (part + step) % head_parts),
+        )
+        copy.start()
+        pending.append(copy)
+    for step in range(1, head_parts):
+        other = (part + step) % head_parts
+        remote(
+            squares.at[other], squares.at[other], sq_send.at[step], sq_recv.at[other], (me, other)
+        ).wait_recv()
+    total = squares[0]
+    for p in range(1, head_parts):
+        total = total + squares[p]
+    inv_rms = lax.rsqrt(total[0:1, :] / WIDTH + EPSILON)
+    inv_rms = jnp.broadcast_to(inv_rms, (BLOCK, HD)).T
+
+    def gram(h):
+        cols = pl.ds(pl.multiple_of(h * HD, HD), HD)
+        normed = mixed[:, cols] * inv_rms * gain_ref[pl.ds(part * heads + h, 1), :]
+        mixed[:, cols] = normed
+        return lax.dot_general(
+            normed,
+            normed,
+            (((0,), (0,)), ((), ())),
+            precision=HIGHEST,
+            preferred_element_type=jnp.float32,
+        )
+
+    def make_pair(p, ref):
+        first, second = gram(2 * p), gram(2 * p + 1)
+        ref[:HD, :] = jnp.where(sub >= lane, first, second)
+        diagonal = jnp.sum(jnp.where(sub == lane, second, 0.0), axis=0, keepdims=True)
+        ref[HD:, :] = jnp.broadcast_to(diagonal, (8, HD))
+
+    def send_pair(step):
+        peer = (me + step) % PEERS
+        return remote(
+            g_send.at[peer], g_recv.at[me], g_send_sem.at[step], g_recv_sem.at[me], (peer, part)
+        )
+
+    def make_and_send(step, carry):
+        peer = (me + step) % PEERS
+        make_pair(peer, g_send.at[peer])
+        send_pair(step).start()
+        return carry
+
+    lax.fori_loop(1, PEERS, make_and_send, 0)
+    make_pair(me, g_recv.at[me])
+    for step in range(1, PEERS):
+        source = (me + step) % PEERS
+        remote(
+            g_recv.at[source], g_recv.at[source], g_send_sem.at[step], g_recv_sem.at[source], (source, part)
+        ).wait_recv()
+    gram_sum = g_recv[0]
+    for s in range(1, PEERS):
+        gram_sum = gram_sum + g_recv[s]
+    body = gram_sum[:HD, :]
+    turned = body.T
+    eye = sub == lane
+    m_ref[0, :, :HD] = jnp.where(sub >= lane, body, turned)
+    m_ref[1, :, :HD] = jnp.where(
+        eye, gram_sum[HD : HD + 1, :], jnp.where(sub < lane, body, turned)
     )
-    return (attn_out, r_factor, whitened)
+    for c in range(2):
+        m_ref[c, :, HD:] = identity()
+    factor(m_ref)
+    for c in range(2):
+        x_buf[me, c] = pack(m_ref[c])
+
+    slot = (lambda owner: x_buf.at[owner], x_send, x_recv)
+    pending += spread(*slot)
+    root = math.sqrt(BLOCK * PEERS)
+
+    def finish(owner):
+        for c in range(2):
+            h = 2 * owner + c
+            cols = pl.ds(pl.multiple_of(h * HD, HD), HD)
+            upper, inverse = unpack(x_buf[owner, c])
+            r_buf[h] = upper * (1.0 / root)
+            white_buf[:, cols] = root * lax.dot_general(
+                mixed[:, cols],
+                inverse,
+                (((1,), (1,)), ((), ())),
+                precision=HIGHEST,
+                preferred_element_type=jnp.float32,
+            )
+
+    finish(me)
+    arrived(*slot, sib)
+    finish(sib)
+    for t in (1, 2, 0):
+        pending.append(forward(*slot, t))
+        finish(near[t])
+    for t in (1, 2, 0):
+        arrived(*slot, near[t] + to_sib)
+        finish(near[t] + to_sib)
+
+    outs = [
+        pltpu.make_async_copy(r_buf, r_hbm, local_sem.at[5]),
+        pltpu.make_async_copy(white_buf, white_hbm, local_sem.at[6]),
+    ]
+    for copy in outs:
+        copy.start()
+    for copy in pending:
+        copy.wait_send()
+    for step in range(1, PEERS):
+        send_pair(step).wait_send()
+    attn_out.wait()
+    for copy in outs:
+        copy.wait()
+
+
+def local_fused(head_parts, queries, keys, values, residual, norm_gain, block_pos, doc_offset):
+    rows, columns = queries.shape
+    heads = columns // HD
+    width = heads // (HEADS // KVH) * HD
+    f32, bf16 = jnp.float32, jnp.bfloat16
+    anywhere = pl.BlockSpec(memory_space=pl.ANY)
+    scalars = pl.BlockSpec(memory_space=pltpu.SMEM)
+    dma = pltpu.SemaphoreType.DMA
+    return pl.pallas_call(
+        functools.partial(fused_kernel, heads, head_parts),
+        in_specs=[anywhere] * 4 + [pl.BlockSpec(memory_space=pltpu.VMEM), scalars, scalars],
+        out_specs=(anywhere,) * 3,
+        out_shape=(
+            jax.ShapeDtypeStruct((rows, columns), bf16),
+            jax.ShapeDtypeStruct((heads, HD, HD), f32),
+            jax.ShapeDtypeStruct((rows, columns), f32),
+        ),
+        scratch_shapes=[
+            pltpu.VMEM((rows, columns), bf16),
+            pltpu.VMEM((rows, columns), bf16),
+            pltpu.VMEM((PEERS * BLOCK, width), bf16),
+            pltpu.VMEM((PEERS * BLOCK, width), bf16),
+            pltpu.VMEM((BLOCK, PEERS * BLOCK), f32),
+            pltpu.VMEM((rows, columns), bf16),
+            pltpu.VMEM((rows, columns), f32),
+            pltpu.VMEM((head_parts, 8, HD), f32),
+            pltpu.VMEM((PEERS, HD + 8, HD), f32),
+            pltpu.VMEM((PEERS, HD + 8, HD), f32),
+            pltpu.VMEM((2, HD, 2 * HD), f32),
+            pltpu.VMEM((PEERS, 2, HD, HD), f32),
+            pltpu.VMEM((heads, HD, HD), f32),
+            pltpu.VMEM((rows, columns), f32),
+            dma((7,)),
+            dma((2, 7)),
+            dma((2, PEERS)),
+            dma((head_parts,)),
+            dma((head_parts,)),
+            dma((PEERS,)),
+            dma((PEERS,)),
+            dma((7,)),
+            dma((PEERS,)),
+        ],
+        compiler_params=pltpu.CompilerParams(
+            collective_id=0, has_side_effects=True, vmem_limit_bytes=40 * 2**20
+        ),
+        name="fused",
+    )(queries, keys, values, residual, norm_gain.reshape(HEADS, HD), block_pos, doc_offset)
 
 
 def solution(mesh):
+    peers, head_parts = mesh.shape["seq"], mesh.shape["head"]
+    if peers == PEERS and HEADS // head_parts == 2 * PEERS:
+        local = functools.partial(local_fused, head_parts)
+    else:
+        local = local_generic
     return jax.shard_map(
         local,
         mesh=mesh,

time: 480 us -> 58.8 us (0.12)
  other arithmetic: 355 us -> 0 us
  waiting for transfers between devices: 54 us -> 0 us
  Pallas kernels: 0 us -> 49.7 us
  blocking collectives: 33.3 us -> 0 us
  between operations: 14.9 us -> 0.66 us
  matrix products: 11 us -> 0 us
    another operation x9 -> x0, other arithmetic: 347 us -> none  [the longest x4 188 us: local(): lower_factor = jnp.linalg.cholesky(gram_sum)]
    psum x1 -> x0, waiting for transfers between devices: 54 us -> none  [local(): gram_sum = lax.psum(gram_of(head_rows), 'seq')]
    pallas_call x0 -> x1, Pallas kernels: none -> 49.7 us  [local_fused(): pl.pallas_call(functools.partial(fused_kernel, heads, head_parts), in_spe...]
    all_gather x2 -> x0, blocking collectives: 21.1 us -> none  [the longest x1 11.3 us: local(): lax.all_gather(key_cols, 'seq', axis=0, tiled=True)]
    psum x1 -> x0, blocking collectives: 12.1 us -> none  [local(): summed = lax.psum(slotted, 'head')]
    dot_general x3 -> x0, matrix products: 9.19 us -> none  [the longest x1 4.89 us: accumulate(): jnp.einsum('kgrn,nkd->kgrd', expo.astype(jnp.bfloat16), value_heads, pref...]
    unnamed x9 -> x17, local copies, waits for them, and re-layouts: 2.82 us -> 8.13 us
  transfers between devices with their start and end apart: 1 -> 0, of which waited for: 1 -> 0; matrix products, arithmetic and copies ran while one was open for 0% -> 0% of each run, Pallas kernels for 0% -> 0%
where the time goes in v1:
time: 58.8 us; the launch traced here: 58.5 us
  Pallas kernels  49.7 us (85%)
  local copies, waits for them, and re-layouts  8.13 us (14%)
  between operations  0.66 us (1%)
    pallas_call x1, Pallas kernels, local_fused(): pl.pallas_call(functools.partial(fused_kernel, heads, head_parts), in_spe...  49.7 us
    unnamed x17, local copies, waits for them, and re-layouts  8.13 us

profile of v1, /device:TPU:0, one launch (start us, length us, event | category | flops | bytes accessed | tf_op | source)
XLA Modules:
  0.0 58.5 jit_solution(14995572165339113480)
XLA Ops:
  0.6 0.0 copy-start.6
  0.6 0.0 copy-start.5
  0.7 0.6 %copy-done.6 = s32[1,8]{1,0:T(1,128)S(1)} copy-done((s32[1,8]{1,0:T(1,128)S(1)}, s32[1,8]{1,0:T(1,128)}, u32[]{:S(2)}) %copy-start.6) | copy-done | bytes 56
  1.3 0.0 copy-done.5
  1.3 0.0 copy-start
  1.3 1.0 %copy-done = bf16[128,2048]{1,0:T(8,128)(2,1)S(1)} copy-done((bf16[128,2048]{1,0:T(8,128)(2,1)S(1)}, bf16[128,2048]{1,0:T(8,128)(2,1)}, u32[]{:S(2)}) %copy-start) | copy-done | bytes 524312
  2.3 0.0 copy-start.1
  2.3 1.0 %copy-done.1 = bf16[128,2048]{1,0:T(8,128)(2,1)S(1)} copy-done((bf16[128,2048]{1,0:T(8,128)(2,1)S(1)}, bf16[128,2048]{1,0:T(8,128)(2,1)}, u32[]{:S(2)}) %copy-start.1) | copy-done | bytes 524312
  3.4 0.0 copy-start.2
  3.4 0.9 %copy-done.2 = bf16[128,1024]{1,0:T(8,128)(2,1)S(1)} copy-done((bf16[128,1024]{1,0:T(8,128)(2,1)S(1)}, bf16[128,1024]{1,0:T(8,128)(2,1)}, u32[]{:S(2)}) %copy-start.2) | copy-done | bytes 262168
  4.3 0.0 copy-start.3
  4.3 0.9 %copy-done.3 = bf16[128,1024]{1,0:T(8,128)(2,1)S(1)} copy-done((bf16[128,1024]{1,0:T(8,128)(2,1)S(1)}, bf16[128,1024]{1,0:T(8,128)(2,1)}, u32[]{:S(2)}) %copy-start.3) | copy-done | bytes 262168
  5.3 0.0 copy-start.4
  5.3 0.8 %copy-done.4 = f32[8192]{0:T(1024)S(1)} copy-done((f32[8192]{0:T(1024)S(1)}, f32[8192]{0:T(1024)}, u32[]{:S(2)}) %copy-start.4) | copy-done | bytes 32792
  6.0 49.7 %fused.1 = (bf16[128,2048]{1,0:T(8,128)(2,1)S(1)}, f32[16,128,128]{2,1,0:T(8,128)S(1)}, f32[128,2048]{1,0:T(8,128)S(1)}) custom-call(bf16[128,2048]{1,0:T(8,128)(2,1)S(1)} %copy-done, bf16[128,1024]{1,0:T(8,128)(2,1)S(1)} %copy-done.2, bf16[128,1024]{1,0:T(8,128)(2,1)S(1)} %copy-done.3, bf16[128,2048]{1,0:T(8,128)(2,1)S(1)} %copy-done.1, ...), custom_call_target="tpu_custom_call" | custom-call | tf_op jit(solution)/shard_map/fused/pallas_call | solution.py:541
  55.7 0.8 %copy.13 = bf16[128,2048]{1,0:T(8,128)(2,1)} copy(bf16[128,2048]{1,0:T(8,128)(2,1)S(1)} %get-tuple-element.6) | data formatting | bytes 1048576
  56.5 1.0 %copy.14 = f32[16,128,128]{2,1,0:T(8,128)} copy(f32[16,128,128]{2,1,0:T(8,128)S(1)} %get-tuple-element.7) | data formatting | bytes 2097152
  57.5 1.0 %copy.15 = f32[128,2048]{1,0:T(8,128)} copy(f32[128,2048]{1,0:T(8,128)S(1)} %get-tuple-element.8) | data formatting | bytes 2097152
Async XLA Ops:
  0.6 0.7 %copy-start.6 = (s32[1,8]{1,0:T(1,128)S(1)}, s32[1,8]{1,0:T(1,128)}, u32[]{:S(2)}) copy-start(s32[1,8]{1,0:T(1,128)} %off_ref.1) | copy-start | bytes 100
  0.6 0.7 %copy-start.5 = (s32[1,8]{1,0:T(1,128)S(1)}, s32[1,8]{1,0:T(1,128)}, u32[]{:S(2)}) copy-start(s32[1,8]{1,0:T(1,128)} %pos_ref.1) | copy-start | bytes 100
  1.3 1.0 %copy-start = (bf16[128,2048]{1,0:T(8,128)(2,1)S(1)}, bf16[128,2048]{1,0:T(8,128)(2,1)}, u32[]{:S(2)}) copy-start(bf16[128,2048]{1,0:T(8,128)(2,1)} %q_ref.1) | copy-start | bytes 1572868
  2.3 1.0 %copy-start.1 = (bf16[128,2048]{1,0:T(8,128)(2,1)S(1)}, bf16[128,2048]{1,0:T(8,128)(2,1)}, u32[]{:S(2)}) copy-start(bf16[128,2048]{1,0:T(8,128)(2,1)} %res_ref.1) | copy-start | bytes 1572868
  3.4 0.9 %copy-start.2 = (bf16[128,1024]{1,0:T(8,128)(2,1)S(1)}, bf16[128,1024]{1,0:T(8,128)(2,1)}, u32[]{:S(2)}) copy-start(bf16[128,1024]{1,0:T(8,128)(2,1)} %k_ref.1) | copy-start | bytes 786436
  4.3 0.9 %copy-start.3 = (bf16[128,1024]{1,0:T(8,128)(2,1)S(1)}, bf16[128,1024]{1,0:T(8,128)(2,1)}, u32[]{:S(2)}) copy-start(bf16[128,1024]{1,0:T(8,128)(2,1)} %v_ref.1) | copy-start | bytes 786436
  5.3 0.8 %copy-start.4 = (f32[8192]{0:T(1024)S(1)}, f32[8192]{0:T(1024)}, u32[]{:S(2)}) copy-start(f32[8192]{0:T(1024)} %param.11) | copy-start | bytes 98308

commit v2 on v1

--- a/solution.py
+++ b/solution.py
@@ -249,26 +249,28 @@
     k_ref,
     v_ref,
     res_ref,
-    gain_ref,
-    pos_ref,
-    off_ref,
-    attn_hbm,
-    r_hbm,
-    white_hbm,
+    gain_hbm,
+    pos_hbm,
+    off_hbm,
+    attn_buf,
+    r_buf,
+    white_buf,
     q_buf,
     res_buf,
     k_buf,
     v_buf,
     bias,
-    attn_buf,
     mixed,
     squares,
     g_send,
     g_recv,
+    g_half,
     m_ref,
-    x_buf,
-    r_buf,
-    white_buf,
+    w_buf,
+    u_buf,
+    gain_ref,
+    pos_ref,
+    off_ref,
     local_sem,
     kv_send,
     kv_recv,
@@ -276,8 +278,12 @@
     sq_recv,
     g_send_sem,
     g_recv_sem,
-    x_send,
-    x_recv,
+    half_send,
+    half_recv,
+    w_send,
+    w_recv,
+    u_send,
+    u_recv,
 ):
     me = lax.axis_index("seq")
     part = lax.axis_index("head")
@@ -300,6 +306,9 @@
         pltpu.make_async_copy(v_ref.at[:, key_cols], v_buf.at[own_rows], local_sem.at[1]),
         pltpu.make_async_copy(q_ref, q_buf, local_sem.at[2]),
         pltpu.make_async_copy(res_ref, res_buf, local_sem.at[3]),
+        pltpu.make_async_copy(pos_hbm, pos_ref, local_sem.at[4]),
+        pltpu.make_async_copy(off_hbm, off_ref, local_sem.at[5]),
+        pltpu.make_async_copy(gain_hbm, gain_ref, local_sem.at[6]),
     ]
     for copy in loads:
         copy.start()
@@ -343,15 +352,35 @@
         copy.start()
         return copy
 
-    def rows_of(buf):
-        return lambda owner: buf.at[pl.ds(pl.multiple_of(owner * BLOCK, BLOCK), BLOCK)]
+    def part_of(buf, share):
+        cols = slice(share * HD, (share + 1) * HD)
+        return lambda owner: buf.at[pl.ds(pl.multiple_of(owner * BLOCK, BLOCK), BLOCK), cols]
 
     pending = []
-    kv = [(rows_of(k_buf), kv_send.at[0], kv_recv.at[0]), (rows_of(v_buf), kv_send.at[1], kv_recv.at[1])]
-    for i, way in enumerate(kv):
-        loads[i].wait()
-        pending += spread(*way)
-
+    kv = [
+        [
+            (part_of(buf, share), kv_send.at[share, i], kv_recv.at[share, i])
+            for i, buf in enumerate((k_buf, v_buf))
+        ]
+        for share in range(shares)
+    ]
+    loads[0].wait()
+    loads[1].wait()
+    for ways in kv:
+        for way in ways:
+            pending += spread(*way)
+
+    def pass_on(share, t):
+        for way in kv[share]:
+            pending.append(forward(*way, t))
+
+    def complete(share):
+        for owner in [sib] + [peer + to_sib for peer in near]:
+            for way in kv[share]:
+                arrived(*way, owner)
+
+    loads[4].wait()
+    loads[5].wait()
     row_pos = pos_ref[0, me]
     lane = iota((BLOCK, BLOCK), 1)
     sub = iota((BLOCK, BLOCK), 0)
@@ -372,14 +401,12 @@
         seen = (key_pos <= own_pos) & (key_doc == own_doc)
         bias[:, s * BLOCK : (s + 1) * BLOCK] = jnp.where(seen, 0.0, -jnp.inf)
 
-    for t in range(3):
-        for way in kv:
-            pending.append(forward(*way, t))
-    for owner in [sib] + [peer + to_sib for peer in near]:
-        for way in kv:
-            arrived(*way, owner)
+    for t in (1, 2, 0):
+        pass_on(0, t)
+    complete(0)
     loads[2].wait()
     loads[3].wait()
+    loads[6].wait()
 
     def attend(h, square):
         cols = pl.ds(pl.multiple_of(h * HD, HD), HD)
@@ -406,11 +433,16 @@
         mixed[:, cols] = mix
         return square + mix * mix
 
-    square = lax.fori_loop(
-        0, heads, attend, jnp.zeros((BLOCK, HD), jnp.float32), unroll=4
-    )
-    attn_out = pltpu.make_async_copy(attn_buf, attn_hbm, local_sem.at[4])
-    attn_out.start()
+    square = jnp.zeros((BLOCK, HD), jnp.float32)
+    for h in range(group // 2):
+        square = attend(h, square)
+    pass_on(1, 1)
+    pass_on(1, 2)
+    for h in range(group // 2, group):
+        square = attend(h, square)
+    pass_on(1, 0)
+    complete(1)
+    square = lax.fori_loop(group, heads, attend, square, unroll=4)
 
     squares[part] = jnp.broadcast_to(jnp.sum(square.T, axis=0, keepdims=True), (8, HD))
     for step in range(1, head_parts):
@@ -452,28 +484,47 @@
         diagonal = jnp.sum(jnp.where(sub == lane, second, 0.0), axis=0, keepdims=True)
         ref[HD:, :] = jnp.broadcast_to(diagonal, (8, HD))
 
-    def send_pair(step):
-        peer = (me + step) % PEERS
-        return remote(
-            g_send.at[peer], g_recv.at[me], g_send_sem.at[step], g_recv_sem.at[me], (peer, part)
-        )
-
-    def make_and_send(step, carry):
-        peer = (me + step) % PEERS
-        make_pair(peer, g_send.at[peer])
-        send_pair(step).start()
-        return carry
-
-    lax.fori_loop(1, PEERS, make_and_send, 0)
-    make_pair(me, g_recv.at[me])
-    for step in range(1, PEERS):
-        source = (me + step) % PEERS
+    chip = me // 2
+    chips = PEERS // 2
+    for k in range(1, chips + 1):
+        target = (chip + k) % chips
+        make_pair(2 * target + 1 - core, g_send.at[target])
+        copy = remote(
+            g_send.at[target], g_half.at[target], half_send.at[k - 1], half_recv.at[target], (sib, part)
+        )
+        copy.start()
+        pending.append(copy)
+
+    def half(target):
         remote(
-            g_recv.at[source], g_recv.at[source], g_send_sem.at[step], g_recv_sem.at[source], (source, part)
+            g_half.at[target], g_half.at[target], half_send.at[0], half_recv.at[target], (sib, part)
+        ).wait_recv()
+        return g_half[target]
+
+    for k in range(1, chips):
+        target = (chip + k) % chips
+        slot = g_send.at[chips + target]
+        make_pair(2 * target + core, slot)
+        slot[...] = slot[...] + half(target)
+        copy = remote(
+            slot, g_recv.at[chip], g_send_sem.at[k], g_recv_sem.at[chip], (2 * target + core, part)
+        )
+        copy.start()
+        pending.append(copy)
+    make_pair(me, g_recv.at[chip])
+    g_recv[chip] = g_recv[chip] + half(chip)
+    for k in range(1, chips):
+        source = (chip + k) % chips
+        remote(
+            g_recv.at[source],
+            g_recv.at[source],
+            g_send_sem.at[k],
+            g_recv_sem.at[source],
+            (2 * source + core, part),
         ).wait_recv()
     gram_sum = g_recv[0]
-    for s in range(1, PEERS):
-        gram_sum = gram_sum + g_recv[s]
+    for c in range(1, chips):
+        gram_sum = gram_sum + g_recv[c]
     body = gram_sum[:HD, :]
     turned = body.T
     eye = sub == lane
@@ -484,50 +535,62 @@
     for c in range(2):
         m_ref[c, :, HD:] = identity()
     factor(m_ref)
-    for c in range(2):
-        x_buf[me, c] = pack(m_ref[c])
-
-    slot = (lambda owner: x_buf.at[owner], x_send, x_recv)
-    pending += spread(*slot)
     root = math.sqrt(BLOCK * PEERS)
 
-    def finish(owner):
-        for c in range(2):
-            h = 2 * owner + c
-            cols = pl.ds(pl.multiple_of(h * HD, HD), HD)
-            upper, inverse = unpack(x_buf[owner, c])
-            r_buf[h] = upper * (1.0 / root)
+    second = m_ref[1, :, HD:]
+    diagonal = jnp.sum(jnp.where(eye, second, 0.0), axis=0, keepdims=True)
+    w_buf[me, :HD, :] = jnp.where(sub >= lane, m_ref[0, :, HD:], second.T)
+    w_buf[me, HD:, :] = jnp.broadcast_to(diagonal, (8, HD))
+    w_way = (lambda owner: w_buf.at[owner], w_send, w_recv)
+    pending += spread(*w_way)
+    second = m_ref[1, :, :HD]
+    diagonal = jnp.sum(jnp.where(eye, second, 0.0), axis=0, keepdims=True)
+    pair = jnp.where(sub <= lane, m_ref[0, :, :HD], second.T)
+    u_buf[me, :HD, :] = (pair * (1.0 / root)).astype(jnp.bfloat16)
+    u_buf[me, HD:, :] = jnp.broadcast_to(diagonal * (1.0 / root), (16, HD)).astype(jnp.bfloat16)
+    u_way = (lambda owner: u_buf.at[owner], u_send, u_recv)
+    pending += spread(*u_way)
+
+    def whiten(owner):
+        body = w_buf[owner, :HD, :]
+        diagonal = w_buf[owner, HD : HD + 1, :]
+        first = jnp.where(sub >= lane, body, 0.0)
+        second = jnp.where(sub < lane, body, jnp.where(eye, diagonal, 0.0))
+        for c, (inverse, side) in enumerate(((first, 1), (second, 0))):
+            cols = pl.ds(pl.multiple_of((2 * owner + c) * HD, HD), HD)
             white_buf[:, cols] = root * lax.dot_general(
                 mixed[:, cols],
                 inverse,
-                (((1,), (1,)), ((), ())),
+                (((1,), (side,)), ((), ())),
                 precision=HIGHEST,
                 preferred_element_type=jnp.float32,
             )
 
-    finish(me)
-    arrived(*slot, sib)
-    finish(sib)
+    def expand(owner):
+        body = u_buf[owner, :HD, :].astype(jnp.float32)
+        diagonal = u_buf[owner, HD:, :].astype(jnp.float32)[0:1, :]
+        r_buf[2 * owner] = jnp.where(sub <= lane, body, 0.0)
+        r_buf[2 * owner + 1] = jnp.where(sub < lane, body.T, jnp.where(eye, diagonal, 0.0))
+
+    whiten(me)
+    arrived(*w_way, sib)
+    whiten(sib)
     for t in (1, 2, 0):
-        pending.append(forward(*slot, t))
-        finish(near[t])
+        pending.append(forward(*w_way, t))
+        whiten(near[t])
+    expand(me)
+    arrived(*u_way, sib)
+    expand(sib)
     for t in (1, 2, 0):
-        arrived(*slot, near[t] + to_sib)
-        finish(near[t] + to_sib)
-
-    outs = [
-        pltpu.make_async_copy(r_buf, r_hbm, local_sem.at[5]),
-        pltpu.make_async_copy(white_buf, white_hbm, local_sem.at[6]),
-    ]
-    for copy in outs:
-        copy.start()
+        pending.append(forward(*u_way, t))
+        arrived(*w_way, near[t] + to_sib)
+        whiten(near[t] + to_sib)
+        expand(near[t])
+    for t in (1, 2, 0):
+        arrived(*u_way, near[t] + to_sib)
+        expand(near[t] + to_sib)
     for copy in pending:
         copy.wait_send()
-    for step in range(1, PEERS):
-        send_pair(step).wait_send()
-    attn_out.wait()
-    for copy in outs:
-        copy.wait()
 
 
 def local_fused(head_parts, queries, keys, values, residual, norm_gain, block_pos, doc_offset):
@@ -535,13 +598,13 @@
     heads = columns // HD
     width = heads // (HEADS // KVH) * HD
     f32, bf16 = jnp.float32, jnp.bfloat16
-    anywhere = pl.BlockSpec(memory_space=pl.ANY)
-    scalars = pl.BlockSpec(memory_space=pltpu.SMEM)
+    outside = pl.BlockSpec(memory_space=pltpu.HBM)
+    inside = pl.BlockSpec(memory_space=pltpu.VMEM)
     dma = pltpu.SemaphoreType.DMA
     return pl.pallas_call(
         functools.partial(fused_kernel, heads, head_parts),
-        in_specs=[anywhere] * 4 + [pl.BlockSpec(memory_space=pltpu.VMEM), scalars, scalars],
-        out_specs=(anywhere,) * 3,
+        in_specs=[outside] * 7,
+        out_specs=(inside,) * 3,
         out_shape=(
             jax.ShapeDtypeStruct((rows, columns), bf16),
             jax.ShapeDtypeStruct((heads, HD, HD), f32),
@@ -553,21 +616,27 @@
             pltpu.VMEM((PEERS * BLOCK, width), bf16),
             pltpu.VMEM((PEERS * BLOCK, width), bf16),
             pltpu.VMEM((BLOCK, PEERS * BLOCK), f32),
-            pltpu.VMEM((rows, columns), bf16),
             pltpu.VMEM((rows, columns), f32),
             pltpu.VMEM((head_parts, 8, HD), f32),
             pltpu.VMEM((PEERS, HD + 8, HD), f32),
+            pltpu.VMEM((PEERS // 2, HD + 8, HD), f32),
+            pltpu.VMEM((PEERS // 2, HD + 8, HD), f32),
+            pltpu.VMEM((2, HD, 2 * HD), f32),
             pltpu.VMEM((PEERS, HD + 8, HD), f32),
-            pltpu.VMEM((2, HD, 2 * HD), f32),
-            pltpu.VMEM((PEERS, 2, HD, HD), f32),
-            pltpu.VMEM((heads, HD, HD), f32),
-            pltpu.VMEM((rows, columns), f32),
+            pltpu.VMEM((PEERS, HD + 16, HD), bf16),
+            pltpu.VMEM((HEADS, HD), f32),
+            pltpu.SMEM((1, PEERS), jnp.int32),
+            pltpu.SMEM((1, PEERS), jnp.int32),
             dma((7,)),
-            dma((2, 7)),
-            dma((2, PEERS)),
+            dma((2, 2, 7)),
+            dma((2, 2, PEERS)),
             dma((head_parts,)),
             dma((head_parts,)),
-            dma((PEERS,)),
+            dma((PEERS // 2,)),
+            dma((PEERS // 2,)),
+            dma((PEERS // 2,)),
+            dma((PEERS // 2,)),
+            dma((7,)),
             dma((PEERS,)),
             dma((7,)),
             dma((PEERS,)),
@@ -576,7 +645,20 @@
             collective_id=0, has_side_effects=True, vmem_limit_bytes=40 * 2**20
         ),
         name="fused",
-    )(queries, keys, values, residual, norm_gain.reshape(HEADS, HD), block_pos, doc_offset)
+    )(
+        *(
+            pltpu.with_memory_space_constraint(x, pltpu.HBM)
+            for x in (
+                queries,
+                keys,
+                values,
+                residual,
+                norm_gain.reshape(HEADS, HD),
+                block_pos,
+                doc_offset,
+            )
+        )
+    )
 
 
 def solution(mesh):

time: 58.8 us -> 48.2 us (0.82)
  local copies, waits for them, and re-layouts: 8.13 us -> 2.73 us
  Pallas kernels: 49.7 us -> 44.7 us
    unnamed x17 -> x3, local copies, waits for them, and re-layouts: 8.13 us -> 2.73 us
    pallas_call x1, Pallas kernels: 49.7 us -> 44.7 us  [local_fused(): pl.pallas_call(functools.partial(fused_kernel, heads, head_parts), in_spe...]
where the time goes in v2:
time: 48.2 us; the launch traced here: 48.1 us
  Pallas kernels  44.7 us (93%)
  local copies, waits for them, and re-layouts  2.73 us (6%)
  between operations  0.64 us (1%)
    pallas_call x1, Pallas kernels, local_fused(): pl.pallas_call(functools.partial(fused_kernel, heads, head_parts), in_spe...  44.7 us
    unnamed x3, local copies, waits for them, and re-layouts  2.73 us

profile of v2, /device:TPU:0, one launch (start us, length us, event | category | flops | bytes accessed | tf_op | source)
XLA Modules:
  0.0 48.1 jit_solution(3170175620846461764)
XLA Ops:
  0.6 44.7 %fused.1 = (bf16[128,2048]{1,0:T(8,128)(2,1)S(1)}, f32[16,128,128]{2,1,0:T(8,128)S(1)}, f32[128,2048]{1,0:T(8,128)S(1)}) custom-call(bf16[128,2048]{1,0:T(8,128)(2,1)} %q_ref.1, bf16[128,1024]{1,0:T(8,128)(2,1)} %k_ref.1, bf16[128,1024]{1,0:T(8,128)(2,1)} %v_ref.1, bf16[128,2048]{1,0:T(8,128)(2,1)} %res_ref.1, f32[64,128]{1,0:T(8,128)} %bitcast.1, ...), custom_call_target="tpu_custom_call" | custom-call | tf_op jit(solution)/shard_map/fused/pallas_call | solution.py:604
  45.3 0.8 %copy.13 = bf16[128,2048]{1,0:T(8,128)(2,1)} copy(bf16[128,2048]{1,0:T(8,128)(2,1)S(1)} %get-tuple-element.6) | data formatting | bytes 1048576
  46.1 1.0 %copy.14 = f32[16,128,128]{2,1,0:T(8,128)} copy(f32[16,128,128]{2,1,0:T(8,128)S(1)} %get-tuple-element.7) | data formatting | bytes 2097152
  47.1 1.0 %copy.15 = f32[128,2048]{1,0:T(8,128)} copy(f32[128,2048]{1,0:T(8,128)S(1)} %get-tuple-element.8) | data formatting | bytes 2097152

commit v3 on v2

--- a/solution.py
+++ b/solution.py
@@ -89,7 +89,20 @@
             )
         return carry
 
-    lax.fori_loop(0, HD // PANEL, panel, 0)
+    lax.fori_loop(0, HD // PANEL, panel, 0, unroll=True)
+
+
+def split(x):
+    high = x.astype(jnp.bfloat16)
+    return (high, (x - high.astype(jnp.float32)).astype(jnp.bfloat16))
+
+
+def product(a, b, dims):
+    (a_high, a_low), (b_high, b_low) = split(a), split(b)
+    dot = functools.partial(
+        lax.dot_general, dimension_numbers=(dims, ((), ())), preferred_element_type=jnp.float32
+    )
+    return dot(a_high, b_high) + (dot(a_high, b_low) + dot(a_low, b_high))
 
 
 def pack(m):
@@ -558,13 +571,7 @@
         second = jnp.where(sub < lane, body, jnp.where(eye, diagonal, 0.0))
         for c, (inverse, side) in enumerate(((first, 1), (second, 0))):
             cols = pl.ds(pl.multiple_of((2 * owner + c) * HD, HD), HD)
-            white_buf[:, cols] = root * lax.dot_general(
-                mixed[:, cols],
-                inverse,
-                (((1,), (side,)), ((), ())),
-                precision=HIGHEST,
-                preferred_element_type=jnp.float32,
-            )
+            white_buf[:, cols] = root * product(mixed[:, cols], inverse, ((1,), (side,)))
 
     def expand(owner):
         body = u_buf[owner, :HD, :].astype(jnp.float32)

time: 48.2 us -> 47.6 us (0.988)
  Pallas kernels: 44.7 us -> 44 us
    pallas_call x1, Pallas kernels: 44.7 us -> 44 us  [local_fused(): pl.pallas_call(functools.partial(fused_kernel, heads, head_parts), in_spe...]
where the time goes in v3:
time: 47.6 us; the launch traced here: 47.4 us
  Pallas kernels  44 us (92%)
  local copies, waits for them, and re-layouts  2.73 us (6%)
  between operations  0.64 us (1%)
    pallas_call x1, Pallas kernels, local_fused(): pl.pallas_call(functools.partial(fused_kernel, heads, head_parts), in_spe...  44 us
    unnamed x3, local copies, waits for them, and re-layouts  2.73 us

profile of v3, /device:TPU:0, one launch (start us, length us, event | category | flops | bytes accessed | tf_op | source)
XLA Modules:
  0.0 47.4 jit_solution(9982786639281113332)
XLA Ops:
  0.6 44.0 %fused.1 = (bf16[128,2048]{1,0:T(8,128)(2,1)S(1)}, f32[16,128,128]{2,1,0:T(8,128)S(1)}, f32[128,2048]{1,0:T(8,128)S(1)}) custom-call(bf16[128,2048]{1,0:T(8,128)(2,1)} %q_ref.1, bf16[128,1024]{1,0:T(8,128)(2,1)} %k_ref.1, bf16[128,1024]{1,0:T(8,128)(2,1)} %v_ref.1, bf16[128,2048]{1,0:T(8,128)(2,1)} %res_ref.1, f32[64,128]{1,0:T(8,128)} %bitcast.1, ...), custom_call_target="tpu_custom_call" | custom-call | tf_op jit(solution)/shard_map/fused/pallas_call | solution.py:611
  44.7 0.8 %copy.13 = bf16[128,2048]{1,0:T(8,128)(2,1)} copy(bf16[128,2048]{1,0:T(8,128)(2,1)S(1)} %get-tuple-element.6) | data formatting | bytes 1048576
  45.5 1.0 %copy.14 = f32[16,128,128]{2,1,0:T(8,128)} copy(f32[16,128,128]{2,1,0:T(8,128)S(1)} %get-tuple-element.7) | data formatting | bytes 2097152
  46.4 1.0 %copy.15 = f32[128,2048]{1,0:T(8,128)} copy(f32[128,2048]{1,0:T(8,128)S(1)} %get-tuple-element.8) | data formatting | bytes 2097152
